TPU v7x, 32 devices: a whole 2x2x4 slice. The times are simulated.
32 devices in a mesh: dp: 8 (over z, x), fsdp: 4 (over y, core).
Axes of the slice: x: 2, y: 2, z: 4, core: 2. Of those that a mesh axis runs over, the one named last changes fastest.
Arguments:
- tokens: bfloat16 [16384, 512], P(('dp', 'fsdp')), may hold values from -6 to 6
- lengths: int32 [32], P(('dp', 'fsdp')), may hold values from 256 to 512, as said below
- norm_gains: bfloat16 [2, 2, 512], P(None, None, ('dp', 'fsdp')), may hold values from 0.5 to 1.5
- norm_shifts: bfloat16 [2, 2, 512], P(None, None, ('dp', 'fsdp')), may hold values from -1.796875 to 1.796875
- w_qkv: bfloat16 [2, 512, 1536], P(None, ('dp', 'fsdp')), may hold values from -0.25 to 0.25
- b_qkv: bfloat16 [2, 1536], P(None, ('dp', 'fsdp')), may hold values from -1.796875 to 1.796875
- w_attn: bfloat16 [2, 512, 512], P(None, ('dp', 'fsdp')), may hold values from -2 to 2
- blend_weights: bfloat16 [2, 3, 512], P(None, None, ('dp', 'fsdp')), may hold values from 0.5 to 1.5
- w_in: bfloat16 [2, 512, 2048], P(None, ('dp', 'fsdp')), may hold values from -0.25 to 0.25
- b_in: bfloat16 [2, 2048], P(None, ('dp', 'fsdp')), may hold values from -1.796875 to 1.796875
- w_out: bfloat16 [2, 2048, 512], P(None, ('dp', 'fsdp')), may hold values from -0.125 to 0.125
- out_bias: bfloat16 [2, 2, 512], P(None, None, ('dp', 'fsdp')), may hold values from -1.796875 to 1.796875
- cotangent: bfloat16 [16384, 512], P(('dp', 'fsdp')), may hold values from -6 to 6
Outputs:
- mixed_out: bfloat16 [16384, 512], P(('dp', 'fsdp'))
- grad_tokens: float32 [16384, 512], P(('dp', 'fsdp'))
- grad_norm_gains: float32 [2, 2, 512], P(None, None, ('dp', 'fsdp'))
- grad_norm_shifts: float32 [2, 2, 512], P(None, None, ('dp', 'fsdp'))
- grad_w_qkv: float32 [2, 512, 1536], P(None, ('dp', 'fsdp'))
- grad_b_qkv: float32 [2, 1536], P(None, ('dp', 'fsdp'))
- grad_w_attn: float32 [2, 512, 512], P(None, ('dp', 'fsdp'))
- grad_blend_weights: float32 [2, 3, 512], P(None, None, ('dp', 'fsdp'))
- grad_w_in: float32 [2, 512, 2048], P(None, ('dp', 'fsdp'))
- grad_b_in: float32 [2, 2048], P(None, ('dp', 'fsdp'))
- grad_w_out: float32 [2, 2048, 512], P(None, ('dp', 'fsdp'))
- grad_out_bias: float32 [2, 2, 512], P(None, None, ('dp', 'fsdp'))
Inputs may be any that keep to these rules, and one draw needn't show every extreme that they name: lengths[i] counts the true tokens of the item on device i, rows 0 to lengths[i] - 1 of its 512 rows; some item has exactly 512 and some exactly 256.
All inputs are finite; a program needn't handle non-finite values.
Results may differ from a plain program's by a relative error of at most 0.015.
Values may be sent and summed in bfloat16 or wider, within the bound.
A program may use at most 192 MiB of HBM per device.

v0:
```python
import functools
import itertools
import jax
import jax.numpy as jnp
from jax import lax
from jax.experimental import pallas as pl
from jax.experimental.pallas import tpu as pltpu
from jax.sharding import PartitionSpec as P

HD = 64
BAND = 30
EPSILON = 1e-05
MESH = pl.DeviceIdType.MESH
F32 = jnp.float32
BF16 = jnp.bfloat16
GROUP = 16
TILE = 128
PAD = 32
WINDOW = TILE + 2 * PAD
TWINS = {"acc_t": "acc", "gm_t": "normed"}
STEP = 2
ROWS = 512
GELU_C = 0.7978845608028654
GELU_A = 0.044715
GAIN, SHIFT, BQKV, BLEND, BIN, OBIAS, VROWS = 0, 2, 4, 7, 10, 14, 16
VECTOR_ROWS = (GAIN, SHIFT, BQKV, BLEND, BIN, OBIAS)


def nn(a, b):
    return jnp.dot(a, b, preferred_element_type=F32)


def nt(a, b):
    return lax.dot_general(a, b, (((1,), (1,)), ((), ())), preferred_element_type=F32)


def split(a):
    high = a.astype(BF16)
    return high, (a - high.astype(F32)).astype(BF16)


def row_index(shape):
    return lax.broadcasted_iota(jnp.int32, shape, 0)


def col_index(shape):
    return lax.broadcasted_iota(jnp.int32, shape, 1)


def head_diag(a):
    return jnp.where((row_index(a.shape) < HD) == (col_index(a.shape) < HD), a, 0.0)


def spread(tile):
    top, bottom = tile[:HD], tile[HD:]
    zero = jnp.zeros_like(top)
    return jnp.concatenate(
        [jnp.concatenate([top, zero], axis=1), jnp.concatenate([zero, bottom], axis=1)], axis=0
    )


def fold(wide):
    half = wide.shape[1] // 2
    return jnp.concatenate([wide[:HD, :half], wide[HD:, half:]], axis=0)


def col_sum(a):
    return jnp.sum(a, axis=0, keepdims=True)


GBLEND = 64


def group_shape(width, hidden):
    first = hidden // width
    return (first, width // GROUP // first // 4, 2, 2)


class Net:
    def __init__(self, layers, seq, width, hidden, length, r):
        self.layers, self.seq, self.width, self.hidden = layers, seq, width, hidden
        self.pairs = width // (2 * HD)
        self.tiles = seq // TILE
        self.length = length
        self.padded = seq + TILE
        self.ff_blocks = hidden // width
        self.groups = group_shape(width, hidden)
        self.__dict__.update(r)
        for name, twin in TWINS.items():
            if name not in r:
                setattr(self, name, r[twin])

    @staticmethod
    def scratch(layers, seq, width, hidden):
        padded = seq + TILE
        pairs = width // (2 * HD)
        tiles = seq // TILE
        ff = hidden // width
        v = pltpu.VMEM
        arrays = dict(
            acc=v((seq, width), F32),
            acc_t=v((width, seq), F32),
            xhat=v((layers, 2, seq, width), BF16),
            rstd=v((seq, 128), F32),
            normed=v((seq, width), BF16),
            normed_t=v((layers, 2, width, seq), BF16),
            q_t=v((layers, width, seq), BF16),
            k_pad=v((layers, padded, width), BF16),
            v_pad=v((layers, padded, width), BF16),
            tr_pad=v((width, padded), BF16),
            probs=v((layers, pairs, tiles, WINDOW, 2 * TILE), BF16),
            near_t=v((layers, width, seq), BF16),
            tanh_t=v((layers, width, seq), BF16),
            s_one=v((layers, pairs, 2 * HD, 2 * HD), F32),
            s_two=v((layers, pairs, 2 * HD, 2 * HD), F32),
            rden=v((layers, pairs, 8, seq), F32),
            mixed_t=v((layers, width, seq), BF16),
            act_t=v((layers, ff, width, seq), BF16),
            dact=v((layers, ff, seq, width), BF16),
            band=v((tiles, WINDOW, 2 * TILE), BF16),
            cols=v((width, 128), F32),
            gm_t=v((width, seq), BF16),
            gk_pad=v((padded, width), F32),
            gv_pad=v((padded, width), F32),
            vecs=v((layers, VROWS, width), F32),
            vgrads=v((layers, VROWS, width), F32),
        )
        return {n: a for n, a in arrays.items() if seq != width or n not in TWINS}

    def w_rows(self, l, first):
        return self.packed[l, :, :, :, :, pl.ds(first, GROUP), :].reshape(self.width, self.width)

    def w_qkv(self, l, n):
        return self.w_rows(l, GROUP * n)

    def w_attn(self, l):
        return self.w_rows(l, 3 * GROUP)

    def w_in(self, l, j):
        return self.w_rows(l, pl.multiple_of(4 * GROUP + GROUP * j, GROUP))

    def out_at(self, j):
        per = self.hidden // (self.width // GROUP)
        return j, pl.ds((4 + self.ff_blocks) * GROUP, per)

    def w_out(self, l, j):
        groups, rows = self.out_at(j)
        return self.packed[l, groups, :, :, :, rows, :].reshape(self.width, self.width)

    def put_rows(self, l, first, value):
        self.grads[:, :, :, :, pl.ds(first, GROUP), :] = value.astype(BF16).reshape(
            self.groups + (GROUP, self.width)
        )

    def put_out(self, l, j, value):
        groups, rows = self.out_at(j)
        per = self.hidden // (self.width // GROUP)
        self.grads[groups, :, :, :, rows, :] = value.astype(BF16).reshape(
            self.groups[1:] + (per, self.width)
        )

    def vec(self, l, row):
        return self.vecs[l, pl.ds(row, 1), :]

    def keep(self, value):
        return jnp.where(row_index(value.shape) < self.length, value, 0.0)

    def setup(self):
        shape = (WINDOW, 2 * TILE)
        key, query = row_index(shape) - PAD, col_index(shape) % TILE
        for t in range(self.tiles):
            pos = key + t * TILE
            ok = (jnp.abs(key - query) <= BAND) & (pos >= 0)
            ok = ok & ((pos < self.length) | (key == query))
            self.band[t] = jnp.where(ok, 0.0, -1e30).astype(BF16)
        zero_head = jnp.zeros((PAD, self.width), BF16)
        zero_tail = jnp.zeros((self.padded - PAD - self.seq, self.width), BF16)
        for l in range(self.layers):
            for ref in (self.k_pad, self.v_pad):
                ref[l, :PAD] = zero_head
                ref[l, PAD + self.seq :] = zero_tail

    def setup_vecs(self):
        eye = (row_index((self.width, self.width)) == col_index((self.width, self.width))).astype(
            BF16
        )
        for l in range(self.layers):
            self.cols[:, VROWS * l : VROWS * (l + 1)] = nt(eye, self.vecs[l].astype(BF16))

    def rows(self, body):
        @pl.loop(0, self.seq // ROWS)
        def _(i):
            body(pl.ds(pl.multiple_of(i * ROWS, ROWS), ROWS))

    def norm(self, l, which, source):
        def body(at):
            value = source[at, :]
            centered = value - jnp.mean(value, axis=-1, keepdims=True)
            rstd = lax.rsqrt(jnp.mean(centered * centered, axis=-1, keepdims=True) + EPSILON)
            xhat = centered * rstd
            n = 2 * l + which
            self.rstd[at, n : n + 1] = rstd
            self.xhat[l, which, at, :] = xhat.astype(BF16)
            normed = xhat * self.vec(l, GAIN + which) + self.vec(l, SHIFT + which)
            self.normed[at, :] = normed.astype(BF16)

        self.rows(body)
        self.normed_t[l, which] = self.normed[...].T

    def pad_keep(self):
        row = row_index((self.padded, 2 * HD)) - PAD
        return (row >= 0) & (row < self.length)

    def fwd_qkv(self, l, n):
        out = (nn(self.normed[...], self.w_qkv(l, n)) + self.vec(l, BQKV + n)).astype(BF16)
        if n == 0:
            self.q_t[l] = out.T
        else:
            (self.k_pad, self.v_pad)[n - 1][l, PAD : PAD + self.seq] = out
        if n == 2:
            self.tr_pad[...] = self.v_pad[l].T

    def pair_at(self, p):
        return pl.ds(pl.multiple_of(p * 2 * HD, 2 * HD), 2 * HD)

    def fwd_near(self, l, p):
        at = self.pair_at(p)
        spans = [
            (slice(t * TILE, (t + 1) * TILE), slice(t * TILE, t * TILE + WINDOW))
            for t in range(self.tiles)
        ]
        scores = [nn(self.k_pad[l, window, at], spread(self.q_t[l, at, here])) for here, window in spans]
        for t, (here, window) in enumerate(spans):
            one = scores[t] * (HD**-0.5) + self.band[t].astype(F32)
            weights = jnp.exp(one - jnp.max(one, axis=0, keepdims=True))
            inverse = 1.0 / jnp.sum(weights, axis=0, keepdims=True)
            probs = (weights * inverse).astype(BF16)
            self.probs[l, p, t] = probs
        for t, (here, window) in enumerate(spans):
            near = fold(nn(self.tr_pad[at, window], self.probs[l, p, t]))
            self.near_t[l, at, here] = near.astype(BF16)

    def features(self, x):
        grown = jnp.exp(jnp.minimum(x, 0.0))
        return jnp.where(x > 0, x + 1.0, grown), grown, jnp.tanh(x)

    def key_features(self, l, at):
        phi, slope, tanh = self.features(self.k_pad[l, :, at].astype(F32))
        ok = self.pad_keep()
        return (
            jnp.where(ok, phi, 0.0).astype(BF16),
            slope,
            jnp.where(ok, tanh, 0.0).astype(BF16),
            tanh,
        )

    def coefficient(self):
        wide = jnp.full((1, 1), HD, F32) * self.length.astype(F32)
        return lax.rsqrt(wide)

    def heads_row(self, two, seq):
        return jnp.concatenate(
            [
                jnp.broadcast_to(two[0:1], (HD, seq)),
                jnp.broadcast_to(two[1:2], (HD, seq)),
            ],
            axis=0,
        )

    def fwd_far(self, l, p):
        at = self.pair_at(p)
        phk, _, tk, _ = self.key_features(l, at)
        values_t = self.tr_pad[at, :]
        s_one = head_diag(nn(values_t, phk))
        s_two = head_diag(nn(values_t, tk))
        total = col_sum(phk.astype(F32))
        self.s_one[l, p], self.s_two[l, p] = s_one, s_two
        phi, _, tanh = self.features(self.q_t[l, at, :].astype(F32))
        phq, tq = phi.astype(BF16), tanh.astype(BF16)
        shape = (8, 2 * HD)
        mine = (row_index(shape) == 0) == (col_index(shape) < HD)
        z_high, z_low = split(jnp.where(mine & (row_index(shape) < 2), total, 0.0))
        den = nn(z_high, phq) + nn(z_low, phq)
        rden = 1.0 / jnp.where(row_index(den.shape) < 2, den, 1.0)
        self.rden[l, p] = rden
        total_col = jnp.broadcast_to(total, (8, 2 * HD)).T
        n = VROWS * l
        self.cols[at, n : n + 1] = total_col[:, 0:1]
        high, low = split(s_one)
        far_elu = (nn(high, phq) + nn(low, phq)) * self.heads_row(rden, self.seq)
        high, low = split(s_two)
        far_tanh = (nn(high, tq) + nn(low, tq)) * self.coefficient()
        self.tanh_t[l, at, :] = far_tanh.astype(BF16)
        blend = self.cols[at, VROWS * l : VROWS * (l + 1)]
        self.mixed_t[l, at, :] = (
            blend[:, BLEND : BLEND + 1] * self.near_t[l, at, :].astype(F32)
            + blend[:, BLEND + 1 : BLEND + 2] * far_elu
            + blend[:, BLEND + 2 : BLEND + 3] * far_tanh
        ).astype(BF16)

    def fwd_attn(self, l):
        mixed = self.mixed_t[l].T
        out = nn(mixed, self.w_attn(l)) + self.vec(l, OBIAS)
        self.gk_pad[: self.seq] = self.h[...] + self.keep(out)
        self.norm(l, 1, self.gk_pad)

    def fwd_up(self, l, j):
        pre = nn(self.normed[...], self.w_in(l, j)) + self.vec(l, BIN + j)
        square = pre * pre
        th = jnp.tanh(GELU_C * pre * (1.0 + GELU_A * square))
        half = 0.5 * (1.0 + th)
        slope = half + (0.5 * GELU_C) * pre * (1.0 - th * th) * (1.0 + 3.0 * GELU_A * square)
        self.dact[l, j] = slope.astype(BF16)
        self.act_t[l, j] = (pre * half).astype(BF16).T

    def fwd_down(self, l):
        self.acc[...] = jnp.broadcast_to(self.vec(l, OBIAS + 1), self.acc.shape)

        @pl.loop(0, self.ff_blocks)
        def _(j):
            self.acc[...] += nn(self.act_t[l, j].T, self.w_out(l, j))

    def fwd_end(self, l):
        self.h[...] = self.gk_pad[: self.seq] + self.keep(self.acc[...])

    def put_vec(self, l, row, value):
        self.vgrads[l, pl.ds(row, 1), :] = value

    def bwd_start(self, l, source):
        gz = self.keep(source[...].astype(F32)).astype(BF16)
        self.normed[...] = gz
        self.put_vec(l, OBIAS + 1, col_sum(gz.astype(F32)))

    def bwd_out(self, l, j):
        self.put_out(l, j, nn(self.act_t[l, j], self.normed[...]))

    def bwd_up(self, l, j):
        grad = nt(self.normed[...], self.w_out(l, j))
        gpre = (grad * self.dact[l, j].astype(F32)).astype(BF16)
        self.put_vec(l, BIN + j, col_sum(gpre.astype(F32)))
        first = pl.multiple_of(4 * GROUP + GROUP * j, GROUP)
        self.put_rows(l, first, nn(self.normed_t[l, 1], gpre))
        self.acc[...] += nt(gpre, self.w_in(l, j))

    def norm_back(self, l, which):
        self.put_vec(l, GAIN + which, jnp.zeros((1, self.width), F32))
        self.put_vec(l, SHIFT + which, jnp.zeros((1, self.width), F32))

        def body(at):
            grad = self.acc[at, :]
            xhat = self.xhat[l, which, at, :].astype(F32)
            self.vgrads[l, pl.ds(GAIN + which, 1), :] += col_sum(grad * xhat)
            self.vgrads[l, pl.ds(SHIFT + which, 1), :] += col_sum(grad)
            grad = grad * self.vec(l, GAIN + which)
            mean = jnp.mean(grad, axis=-1, keepdims=True)
            slope = jnp.mean(grad * xhat, axis=-1, keepdims=True)
            n = 2 * l + which
            self.h[at, :] += self.rstd[at, n : n + 1] * (grad - mean - xhat * slope)

        self.rows(body)

    def bwd_attn(self, l):
        self.norm_back(l, 1)
        go = self.keep(self.h[...]).astype(BF16)
        self.put_vec(l, OBIAS, col_sum(go.astype(F32)))
        self.put_rows(l, 3 * GROUP, nn(self.mixed_t[l], go))
        self.gm_t[...] = nt(self.w_attn(l), go).astype(BF16)
        self.tr_pad[...] = self.k_pad[l].T
        self.gk_pad[...] = jnp.zeros_like(self.gk_pad)
        self.gv_pad[...] = jnp.zeros_like(self.gv_pad)

    def bwd_near(self, l, p):
        at = self.pair_at(p)
        blend = self.cols[at, VROWS * l : VROWS * (l + 1)]
        spans = [
            (slice(t * TILE, (t + 1) * TILE), slice(t * TILE, t * TILE + WINDOW))
            for t in range(self.tiles)
        ]
        grads = []
        for here, _ in spans:
            grad = blend[:, BLEND : BLEND + 1] * self.gm_t[at, here].astype(F32)
            grads.append(spread(grad.astype(BF16)))
        dprobs = [nn(self.v_pad[l, window, at], g) for g, (_, window) in zip(grads, spans)]
        terms = []
        for t in range(self.tiles):
            wide = self.probs[l, p, t].astype(F32)
            term = wide * dprobs[t]
            inner = jnp.sum(term, axis=0, keepdims=True)
            terms.append(((term - wide * inner) * (HD**-0.5)).astype(BF16))
        for gs, (here, window) in zip(terms, spans):
            self.acc_t[at, here] = fold(nn(self.tr_pad[at, window], gs))
        keys = [nt(gs, spread(self.q_t[l, at, here])) for gs, (here, _) in zip(terms, spans)]
        values = [nt(self.probs[l, p, t], grads[t]) for t in range(self.tiles)]
        for t, (_, window) in enumerate(spans):
            self.gk_pad[window, at] += keys[t]
            self.gv_pad[window, at] += values[t]

    def bwd_far(self, l, p):
        at = self.pair_at(p)
        seq = self.seq
        blend = self.cols[at, VROWS * l : VROWS * (l + 1)]
        gm = self.gm_t[at, :].astype(F32)
        q = self.q_t[l, at, :].astype(F32)
        phi_q, slope_q, tanh_q = self.features(q)
        phq, tq = phi_q.astype(BF16), tanh_q.astype(BF16)
        high, low = split(self.s_one[l, p])
        far_elu = (nn(high, phq) + nn(low, phq)) * self.heads_row(self.rden[l, p], seq)
        column = lambda a: jnp.sum(a, axis=1, keepdims=True)
        sums = [
            column(gm * self.near_t[l, at, :].astype(F32)),
            column(gm * far_elu),
            column(gm * self.tanh_t[l, at, :].astype(F32)),
        ]
        for n, one in enumerate(sums):
            self.cols[at, GBLEND + n : GBLEND + n + 1] = one
        phk, slope_k, tk, tanh_k = self.key_features(l, at)
        values = self.v_pad[l, :, at]
        gnum = (blend[:, BLEND + 1 : BLEND + 2] * gm * self.heads_row(self.rden[l, p], seq)).astype(
            BF16
        )
        prod = gnum.astype(F32) * far_elu
        gden_one = -col_sum(prod[:HD])
        gden_two = -col_sum(prod[HD:])
        gden = jnp.concatenate([gden_one, gden_two, jnp.zeros((6, seq), F32)], axis=0)
        s_one = self.s_one[l, p].T
        high, low = split(s_one)
        gphq = nn(high, gnum) + nn(low, gnum) + self.cols[at, VROWS * l : VROWS * l + 1] * self.heads_row(gden, seq)
        gs_one = head_diag(nt(phq, gnum))
        gs_high, gs_low = split(gs_one)
        gden_high, gden_low = split(gden)
        both = nt(gden_high, phq) + nt(gden_low, phq)
        gzz = jnp.where(col_index((1, 2 * HD)) < HD, both[0:1], both[1:2])
        gtanh = (blend[:, BLEND + 2 : BLEND + 3] * gm * self.coefficient()).astype(BF16)
        gtq = nn(self.s_two[l, p].T.astype(BF16), gtanh)
        gs_two = head_diag(nt(tq, gtanh)).astype(BF16)
        self.acc_t[at, :] += gphq * jnp.where(q > 0, 1.0, slope_q) + gtq * (1.0 - tanh_q * tanh_q)
        gphk = nt(values, gs_high) + nt(values, gs_low) + gzz
        gtk = nt(values, gs_two)
        grad_k = gphk * slope_k + gtk * (1.0 - tanh_k * tanh_k)
        self.gk_pad[:, at] += jnp.where(self.pad_keep(), grad_k, 0.0)
        self.gv_pad[:, at] += nn(phk, gs_high) + nn(tk, gs_two)

    def bwd_qkv(self, l, n):
        rows = slice(PAD, PAD + self.seq)
        if n == 0:
            grad = self.acc_t[...].T.astype(BF16)
        else:
            grad = (self.gk_pad, self.gv_pad)[n - 1][rows, :].astype(BF16)
        self.put_vec(l, BQKV + n, col_sum(grad.astype(F32)))
        self.put_rows(l, GROUP * n, nn(self.normed_t[l, 0], grad))
        total = self.gv_pad.at[rows]
        part = nt(grad, self.w_qkv(l, n))
        if n == 2:
            total[...] = part
        elif n == 1:
            total[...] += part
        else:
            self.acc[...] = total[...] + part

    def bwd_end(self, l):
        self.vgrads[l, pl.ds(BLEND, 3), :] = self.cols[...].T[GBLEND : GBLEND + 3]
        self.norm_back(l, 0)


class Comm:
    def __init__(self, depth, sems):
        self.sems = sems
        self.free = ([], [])
        self.made = [0, 0]
        self.clock = 0
        self.heard = {}
        dp, fsdp = lax.axis_index("dp"), lax.axis_index("fsdp")
        self.depth = depth
        self.at = {"z": dp // 2, "x": dp % 2, "y": fsdp // 2, "c": fsdp % 2}

    def device(self, **moved):
        at = dict(self.at, **moved)
        return (at["z"] * 2 + at["x"], at["y"] * 2 + at["c"])

    def steps(self, axis):
        return range(1, self.depth) if axis == "z" else range(1, 2)

    def other(self, axis, step=1):
        if axis == "z":
            return lax.rem(self.at["z"] + step, self.depth)
        return 1 - self.at[axis]

    def barrier(self):
        semaphore = pltpu.get_barrier_semaphore()
        peers = [
            self.device(**{axis: self.other(axis, k)}) for axis in "zxyc" for k in self.steps(axis)
        ]
        for peer in peers:
            pl.semaphore_signal(semaphore, inc=1, device_id=peer, device_id_type=MESH)
        pl.semaphore_wait(semaphore, len(peers))

    def take(self, side, before):
        for entry in self.free[side]:
            if entry[0] < before:
                self.free[side].remove(entry)
                return entry[1]
        self.made[side] += 1
        return self.made[side] - 1

    def copy(self, source, target, axis, step):
        self.clock += 1
        sent = self.take(0, self.clock)
        arrived = self.take(1, self.heard.get((axis, step), -1))
        made = pltpu.make_async_remote_copy(
            src_ref=source,
            dst_ref=target,
            send_sem=self.sems[0].at[sent],
            recv_sem=self.sems[1].at[arrived],
            device_id=self.device(**{axis: self.other(axis, step)}),
            device_id_type=MESH,
        )
        made.start()
        back = (axis, self.depth - step if axis == "z" else 1)
        return made, sent, arrived, back, self.clock

    def wait(self, copies):
        for made, sent, arrived, back, when in copies:
            made.wait()
            self.clock += 1
            self.free[0].append((self.clock, sent))
            self.free[1].append((self.clock, arrived))
            self.heard[back] = max(when, self.heard.get(back, -1))

    def index(self, whole, moved=None):
        at = dict(self.at, **(moved or {}))
        return tuple(slice(None) if axis in whole else at[axis] for axis in "zxyc")

    def gather(self, view, order):
        cores = []
        for stage in range(4):
            whole, started = order[:stage], []
            if stage < 3:
                axis = order[stage]
                block = view(self.index(whole))
                started = [self.copy(block, block, axis, k) for k in self.steps(axis)]
            if "z" in whole:
                axis = order[stage - 1]
                if axis == "z":
                    block = view(self.index(whole))
                else:
                    block = view(self.index(order[: stage - 1], {axis: self.other(axis)}))
                cores.append(self.copy(block, block, "c", 1))
            yield
            self.wait(started)
        self.wait(cores)

    @staticmethod
    def add(mine, others):
        @pl.loop(0, mine.shape[0])
        def _(n):
            for rest in itertools.product(*[range(m) for m in mine.shape[1:-2]]):
                at = (n,) + rest
                total = mine[at]
                for other in others:
                    total = total + other[at]
                mine[at] = total

    def scatter(self, view, slot, order, put):
        axes = "c" + order
        for stage, axis in enumerate(axes):
            whole = axes[stage + 1 :]
            started = []
            for k in self.steps(axis):
                block = view(self.index(whole, {axis: self.other(axis, k)}))
                started.append(self.copy(block, slot(stage, k - 1), axis, k))
            yield
            self.wait(started)
            mine = view(self.index(whole))
            arrived = [slot(stage, k - 1) for k in self.steps(axis)]
            if whole:
                self.add(mine, arrived)
            else:
                total = mine[...].astype(F32)
                for one in arrived:
                    total = total + one[...].astype(F32)
                put(total)


ORDERS = {
    ("gather", 0): (
        "xzy", "zyx", "zxy", "zyx", "yzx", "zxy",
        "zyx", "zxy", "zyx", "zxy", "zyx", "zxy",
    ),
    ("gather", 1): (
        "zyx", "xzy", "yzx", "yzx", "zyx", "xzy",
        "yzx", "zxy", "zyx", "zyx", "xzy", "xzy",
    ),
    ("scatter", 0): (
        "xyz", "xyz", "yzx", "xyz", "xyz", "yxz",
        "xyz", "yxz", "xzy", "yzx", "yzx", "xyz",
    ),
    ("scatter", 1): (
        "yxz", "xzy", "yzx", "yxz", "xzy", "yzx",
        "xyz", "xyz", "xyz", "xyz", "yzx", "yzx",
    ),
}
LINK, HOP = 0.0235, 1.8
CORE, CORE_HOP = 0.0027, 0.9
ISSUE, BACKLOG, AHEAD = 0.04, 6.0, 12


def plan(layers, segments, parts):
    size = {"z": 4, "x": 2, "y": 2, "c": 2}
    free = dict.fromkeys("zxyc", 0.0)
    clock, steps = 0.0, []
    stage = dict.fromkeys(parts, 0)
    ready = {n: 0.0 if not scatter else None for n, (_, _, scatter) in parts.items()}
    done = set()
    waiting = list(segments)

    def send(axis, blocks, rows):
        link, hop = (CORE, CORE_HOP) if axis == "c" else (LINK, HOP)
        load = blocks * rows * link * (size["z"] if axis == "z" else 1)
        free[axis] = max(free[axis], clock) + load
        return free[axis] + hop

    def count(axes):
        total = 1
        for axis in axes:
            total *= size[axis]
        return total

    def step(name):
        nonlocal clock
        rows, order, scatter = parts[name]
        now = stage[name]
        steps.append((name,))
        stage[name] += 1
        last = 4
        if scatter:
            axes = "c" + order
            if now > 0:
                clock += 0.02 + count(axes[now:]) * rows * 0.0002
            if now < last:
                arrives = send(axes[now], count(axes[now + 1 :]), rows)
                clock += ISSUE * (3 if axes[now] == "z" else 1)
        else:
            arrives = ready[name]
            if now < 3:
                arrives = send(order[now], count(order[:now]), rows)
                clock += ISSUE * (3 if order[now] == "z" else 1)
            if "z" in order[:now] and now < last:
                whole = order[:now] if order[now - 1] == "z" else order[: now - 1]
                core = send("c", count(whole), rows)
                clock += ISSUE
                if now == 3:
                    arrives = core
        if now == last:
            done.add(name)
            ready[name] = None
        else:
            ready[name] = arrives

    def startable(name):
        _, order, scatter = parts[name]
        first = "c" if scatter else order[0]
        return stage[name] > 0 or free[first] <= clock + BACKLOG

    while len(done) < len(parts) or waiting:
        left = [n for n in parts if n not in done][:AHEAD]
        able = [n for n in left if ready[n] is not None and ready[n] <= clock and startable(n)]
        if able:
            step(able[0])
            continue
        if waiting:
            name, layer, argument, cost, needs, makes = waiting[0]
            if all(n in done for n in needs):
                waiting.pop(0)
                steps.append((name, layer, argument))
                clock += cost
                for n in makes:
                    ready[n] = clock
                continue
        later = [ready[n] for n in left if ready[n] is not None and ready[n] > clock]
        later += [free[a] - BACKLOG for a in "zxyc" if free[a] - BACKLOG > clock]
        clock = min(later)
    return steps, clock


def make_plan(layers, pairs, ff, rows):
    units = rows // GROUP
    parts = {("gather", 0, "vectors"): (4, "zxy", False)}
    for l in range(layers):
        for u in range(units):
            parts["gather", l, u] = (GROUP, ORDERS["gather", l][u], False)
    late = list(range(units - ff, units)) + list(range(4, units - ff)) + [3, 2, 1, 0]
    for l in reversed(range(layers)):
        for u in late:
            parts["scatter", l, u] = (GROUP, ORDERS["scatter", l][u], True)
    parts["scatter", 0, "vectors"] = (8, "yxz", True)
    gathers = lambda l, us: [("gather", l, u) for u in us]
    scatters = lambda l, us: [("scatter", l, u) for u in us]
    downs = range(units - ff, units)
    segments = []
    add = lambda *s: segments.append(s)
    halves = [(0, pairs)]
    twos = [(j, min(j + STEP, ff)) for j in range(0, ff, STEP)]
    add("start", 0, None, 0.5, [], [])
    add("spread", 0, None, 0.5, [("gather", 0, "vectors")], [])
    for l in range(layers):
        add("norm", l, 0, 0.7, [], [])
        for n in range(3):
            add("fwd_qkv", l, n, 0.25, gathers(l, [n]), [])
        for half in halves:
            add("fwd_near", l, half, 2.6, [], [])
        for half in halves:
            add("fwd_far", l, half, 2.3, [], [])
        add("fwd_attn", l, None, 1.3, gathers(l, [3]), [])
        for j, end in twos:
            add("fwd_up", l, (j, end), 1.05 * (end - j), gathers(l, range(4 + j, 4 + end)), [])
        if l == layers - 1:
            add("bwd_start", l, None, 0.3, [], [])
            add("bwd_out", l, (0, ff), 0.43 * ff, [], scatters(l, downs))
        add("fwd_down", l, None, 1.9, gathers(l, downs), [])
    for l in reversed(range(layers)):
        again = lambda us: scatters(l + 1, us) if l < layers - 1 else []
        if l < layers - 1:
            add("bwd_start", l, None, 0.3, [], [])
            add("bwd_out", l, (0, ff), 0.43 * ff, again(downs), scatters(l, downs))
        for j, end in twos:
            units = range(4 + j, 4 + end)
            add("bwd_up", l, (j, end), 1.33 * (end - j), again(units), scatters(l, units))
        add("bwd_attn", l, None, 1.6, again([3]), scatters(l, [3]))
        for half in halves:
            add("bwd_near", l, half, 3.1, [], [])
        for half in halves:
            add("bwd_far", l, half, 3.8, [], [])
        for n in (2, 1, 0):
            add("bwd_qkv", l, n, 0.6, again([n]), scatters(l, [n]))
        add("bwd_end", l, None, 0.9, [], [])
    add("collect", 0, None, 0.5, [], scatters(0, ["vectors"]))
    return plan(layers, segments, parts), parts


class Vectors:
    def __init__(self, layers, width, hidden):
        self.layers, self.width = layers, width
        self.devices = width // GROUP
        self.long = [(BQKV, 3), (BIN, hidden // width)]

    def swap(self, tiles, back):
        lane = lax.broadcasted_iota(jnp.int32, tiles.shape, 2)
        result = tiles
        for l in range(self.layers):
            for row, count in self.long:
                first = l * VROWS + row
                columns = [tiles[:, :, first + n : first + n + 1] for n in range(count)]
                if back:
                    both = jnp.stack(columns, axis=1).reshape(count, self.devices, GROUP, 1)
                    columns = [both[n] for n in range(count)]
                else:
                    both = jnp.concatenate(columns, axis=0)
                    both = both.reshape(self.devices, count, GROUP, 1)
                    columns = [both[:, n] for n in range(count)]
                for n in range(count):
                    result = jnp.where(lane == first + n, columns[n], result)
        return result

    def spread(self, shares, vecs, cols):
        tiles = shares[...].reshape(self.devices, GROUP, 128).astype(F32)
        columns = self.swap(tiles, True).reshape(self.width, 128)
        cols[...] = columns
        vecs[...] = columns.T[: self.layers * VROWS].reshape(vecs.shape)

    def collect(self, vgrads, shares):
        rows = vgrads[...].reshape(self.layers * VROWS, self.width)
        rest = jnp.zeros((128 - self.layers * VROWS, self.width), F32)
        columns = jnp.concatenate([rows, rest], axis=0).T
        tiles = self.swap(columns.reshape(self.devices, GROUP, 128), False)
        shares[...] = tiles.reshape(shares.shape)

    def pack(self, refs, table):
        table[...] = jnp.zeros_like(table)
        for l in range(self.layers):
            for ref, row in zip(refs, VECTOR_ROWS):
                row += l * VROWS
                if len(ref.shape) == 3:
                    table[row : row + ref.shape[1], :GROUP] = ref[l].astype(F32)
                else:
                    value = ref[l : l + 1, :].astype(F32)
                    for n in range(ref.shape[1] // GROUP):
                        piece = value[:, n * GROUP : (n + 1) * GROUP]
                        table[row + n : row + n + 1, :GROUP] = piece
        return table[...].T[:GROUP]

    def unpack(self, tile, table, refs):
        rest = jnp.zeros((128 - GROUP, 128), F32)
        table[...] = jnp.concatenate([tile, rest], axis=0).T
        for l in range(self.layers):
            for ref, row in zip(refs, VECTOR_ROWS):
                row += l * VROWS
                if len(ref.shape) == 3:
                    ref[l] = table[row : row + ref.shape[1], :GROUP]
                else:
                    count = ref.shape[1] // GROUP
                    rows = [table[row + n : row + n + 1, :GROUP] for n in range(count)]
                    ref[l : l + 1, :] = jnp.concatenate(rows, axis=1)


class Program:
    def __init__(self, net, comm, vectors, r):
        self.net, self.comm, self.vectors = net, comm, vectors
        self.__dict__.update(r)

    def fill(self):
        own = self.comm.index(())
        width = self.net.width
        for l in range(self.net.layers):
            first = 0
            for ref in (self.w_qkv, self.w_attn, self.w_in):
                for n in range(ref.shape[2] // width):
                    rows = pl.ds(first, GROUP)
                    self.net.packed[(l,) + own + (rows,)] = ref[l, :, n * width : (n + 1) * width]
                    first += GROUP
            rows = pl.ds(first, self.w_out.shape[1])
            self.net.packed[(l,) + own + (rows,)] = self.w_out[l]
        refs = [getattr(self, name) for name in VECTORS]
        self.shares[own] = self.vectors.pack(refs, self.table).astype(BF16)

    def gather(self, l, unit, order):
        if unit == "vectors":
            return self.comm.gather(lambda index: self.shares.at[index], order)
        at = pl.ds(unit * GROUP, GROUP)
        return self.comm.gather(lambda index: self.net.packed.at[(l,) + index + (at,)], order)

    def scatter(self, l, unit, order):
        if unit == "vectors":
            arrivals, at, source = self.varrivals, (), self.vshares
        else:
            at = (pl.ds(unit * GROUP, GROUP),)
            arrivals, source = self.arrivals, self.net.grads
        depth = self.comm.depth
        every = slice(None)

        def slot(stage, k):
            if stage < 2:
                return arrivals[stage].at[(every,) * (3 - stage) + at]
            if stage == 2:
                span = slice(2 * k, 2 * k + 2) if order[1] == "z" else slice(0, depth)
                return arrivals[2].at[(span,) + at]
            return arrivals[2].at[(2 * (depth - 1) if order[1] == "z" else depth + k,) + at]

        put = functools.partial(self.put, l, unit)
        return self.comm.scatter(lambda index: source.at[index + at], slot, order, put)

    def put(self, l, unit, total):
        if unit == "vectors":
            self.gsmall[...] = total
            return
        width = self.net.width
        for ref in (self.gw_qkv, self.gw_attn, self.gw_in):
            count = ref.shape[2] // width
            if unit < count:
                ref[l, :, unit * width : (unit + 1) * width] = total
                return
            unit -= count
        self.gw_out[l, unit * GROUP : (unit + 1) * GROUP, :] = total

    def start(self, l, _):
        self.net.setup()
        self.net.h[...] = self.tokens[...].astype(F32)

    def spread(self, l, _):
        self.vectors.spread(self.shares, self.net.vecs, self.net.cols)

    def collect(self, l, _):
        self.vectors.collect(self.net.vgrads, self.vshares)

    def norm(self, l, _):
        self.net.norm(l, 0, self.net.h)

    def fwd_attn(self, l, _):
        self.net.fwd_attn(l)

    def fwd_down(self, l, _):
        self.net.fwd_down(l)
        self.net.fwd_end(l)
        if l == self.net.layers - 1:
            self.mixed_out[...] = self.net.h[...].astype(BF16)
            self.net.h[...] = self.cotangent[...].astype(F32)

    def bwd_up(self, l, span):
        if span[0] == 0:
            self.net.acc[...] = jnp.zeros_like(self.net.acc)
        self.over(self.net.bwd_up, l, span)

    def bwd_start(self, l, _):
        self.net.bwd_start(l, self.cotangent if l == self.net.layers - 1 else self.net.h)

    def bwd_attn(self, l, _):
        self.net.bwd_attn(l)

    def bwd_end(self, l, _):
        self.net.bwd_end(l)

    def over(self, body, l, span):
        @pl.loop(*span)
        def _(p):
            body(l, p)

    def run(self):
        net = self.net
        rows = net.packed.shape[-2]
        (steps, _), parts = make_plan(net.layers, net.pairs, net.ff_blocks, rows)
        running = {}
        for (kind, l, unit), (_, order, _) in parts.items():
            make = self.gather if kind == "gather" else self.scatter
            running[kind, l, unit] = make(l, unit, order)
        self.fill()
        self.comm.barrier()
        for name, *rest in steps:
            if not rest:
                next(running[name], None)
            elif hasattr(self, name):
                getattr(self, name)(*rest)
            elif isinstance(rest[1], tuple):
                self.over(getattr(net, name), *rest)
            else:
                getattr(net, name)(*rest)
        assert max(self.comm.made) <= SEMAPHORES


VECTORS = ("gains", "shifts", "b_qkv", "blends", "b_in", "biases")
WEIGHTS = ("w_qkv", "w_attn", "w_in", "w_out")
INPUTS = ("tokens", "cotangent") + VECTORS + WEIGHTS
OUTPUTS = ("mixed_out", "h", "gsmall", "gw_qkv", "gw_attn", "gw_in", "gw_out")
SEMAPHORES = 96


def fused_body(sizes, depth, names, length_ref, *refs):
    named = dict(zip(INPUTS + OUTPUTS + names, refs))
    arrivals = [named.pop("arrive%d" % n) for n in range(3)]
    varrivals = [named.pop("varrive%d" % n) for n in range(3)]
    sems = named.pop("send"), named.pop("recv")
    inner = {n: r for n, r in named.items() if n not in INPUTS}
    net = Net(*sizes, length_ref[0], inner)
    comm = Comm(depth, sems)
    vectors = Vectors(sizes[0], sizes[2], sizes[3])
    Program(net, comm, vectors, dict(named, arrivals=arrivals, varrivals=varrivals)).run()


def fused(lengths, tokens, cotangent, vectors, weights):
    layers, _, width = weights[1].shape
    hidden = weights[2].shape[2]
    seq = tokens.shape[0]
    sizes = (layers, seq, width, hidden)
    rows = sum(w.shape[1] * w.shape[2] for w in weights) // width
    groups = group_shape(width, hidden)
    tile = (GROUP, 128)
    vmem = pl.BlockSpec(memory_space=pltpu.VMEM)
    scratch = dict(Net.scratch(*sizes))
    scratch["packed"] = pltpu.VMEM((layers,) + groups + (rows, width), BF16)
    scratch["grads"] = pltpu.VMEM(groups + (rows, width), BF16)
    scratch["shares"] = pltpu.VMEM(groups + tile, BF16)
    scratch["vshares"] = pltpu.VMEM(groups + tile, F32)
    scratch["table"] = pltpu.VMEM((128, 128), F32)
    kept = (groups[:3], groups[:2], (2 * groups[0] - 1,))
    for n, lead in enumerate(kept):
        scratch["arrive%d" % n] = pltpu.VMEM(lead + (rows, width), BF16)
        scratch["varrive%d" % n] = pltpu.VMEM(lead + tile, F32)
    scratch["send"] = pltpu.SemaphoreType.DMA((SEMAPHORES,))
    scratch["recv"] = pltpu.SemaphoreType.DMA((SEMAPHORES,))
    return pl.pallas_call(
        functools.partial(fused_body, sizes, groups[0], tuple(scratch)),
        out_shape=(
            jax.ShapeDtypeStruct(tokens.shape, BF16),
            jax.ShapeDtypeStruct(tokens.shape, F32),
            jax.ShapeDtypeStruct(tile, F32),
        )
        + tuple(jax.ShapeDtypeStruct(w.shape, F32) for w in weights),
        in_specs=[pl.BlockSpec(memory_space=pltpu.SMEM)] + [vmem] * len(INPUTS),
        out_specs=(vmem,) * len(OUTPUTS),
        scratch_shapes=list(scratch.values()),
        compiler_params=pltpu.CompilerParams(
            collective_id=0, has_side_effects=True, vmem_limit_bytes=63 * 2**20
        ),
    )(lengths, tokens, cotangent, *vectors, *weights)


def finish_body(vectors, big, *refs):
    sources, tile, refs = refs[:big], refs[big], refs[big + 1 :]
    targets, outs, table, sems = refs[:big], refs[big : -big - 2], refs[-big - 2], refs[-big - 1]
    buffers = refs[-big:]
    loads = [
        pltpu.make_async_copy(source, buffer, sems.at[0, n])
        for n, (source, buffer) in enumerate(zip(sources, buffers))
    ]
    stores = [
        pltpu.make_async_copy(buffer, target, sems.at[1, n])
        for n, (buffer, target) in enumerate(zip(buffers, targets))
    ]
    for one in loads:
        one.start()
    vectors.unpack(tile[...], table, outs)
    for load, store in zip(loads, stores):
        load.wait()
        store.start()
    for one in stores:
        one.wait()


def finish(vectors, large, tile, shapes):
    anywhere, vmem = pl.BlockSpec(memory_space=pl.ANY), pl.BlockSpec(memory_space=pltpu.VMEM)
    outs = pl.pallas_call(
        functools.partial(finish_body, vectors, len(large)),
        out_shape=tuple(jax.ShapeDtypeStruct(a.shape, a.dtype) for a in large)
        + tuple(jax.ShapeDtypeStruct(shape, F32) for shape in shapes),
        in_specs=[anywhere] * len(large) + [vmem],
        out_specs=(anywhere,) * len(large) + (vmem,) * len(shapes),
        scratch_shapes=[
            pltpu.VMEM((128, 128), F32),
            pltpu.SemaphoreType.DMA((2, len(large))),
        ]
        + [pltpu.VMEM(a.shape, a.dtype) for a in large],
        compiler_params=pltpu.CompilerParams(vmem_limit_bytes=62 * 2**20),
    )(*large, tile)
    return outs[: len(large)], outs[len(large) :]


def plain_body(sizes, names, length_ref, *refs):
    names = ("tokens", "cotangent", "packed", "vecs", "mixed_out", "h", "grads_out", "vgrads") + names
    named = dict(zip(names, refs))
    net = Net(*sizes, length_ref[0], named)

    def over(body, l):
        @pl.loop(0, net.pairs)
        def _(p):
            body(l, p)

    net.setup()
    net.setup_vecs()
    net.h[...] = named["tokens"][...].astype(F32)
    for l in range(net.layers):
        net.norm(l, 0, net.h)
        for n in range(3):
            net.fwd_qkv(l, n)
        over(net.fwd_near, l)
        over(net.fwd_far, l)
        net.fwd_attn(l)
        for j in range(net.ff_blocks):
            net.fwd_up(l, j)
        net.fwd_down(l)
        net.fwd_end(l)
    named["mixed_out"][...] = net.h[...].astype(BF16)
    net.h[...] = named["cotangent"][...].astype(F32)
    for l in reversed(range(net.layers)):
        net.bwd_start(l, net.h)
        net.acc[...] = jnp.zeros_like(net.acc)
        for j in range(net.ff_blocks):
            net.bwd_out(l, j)
            net.bwd_up(l, j)
        net.bwd_attn(l)
        over(net.bwd_near, l)
        over(net.bwd_far, l)
        for n in (2, 1, 0):
            net.bwd_qkv(l, n)
        net.bwd_end(l)
        copy = pltpu.make_async_copy(named["grads"], named["grads_out"].at[l], named["sem"])
        copy.start()
        copy.wait()


def plain(lengths, tokens, cotangent, packed, vecs):
    layers, rows, width = packed.shape[0], packed.shape[-2], packed.shape[-1]
    seq = tokens.shape[0]
    hidden = (rows // GROUP - 4) // 2 * width
    sizes = (layers, seq, width, hidden)
    scratch = dict(Net.scratch(*sizes))
    del scratch["vecs"], scratch["vgrads"]
    scratch["grads"] = pltpu.VMEM(packed.shape[1:], BF16)
    scratch["sem"] = pltpu.SemaphoreType.DMA
    vmem = pl.BlockSpec(memory_space=pltpu.VMEM)
    return pl.pallas_call(
        functools.partial(plain_body, sizes, tuple(scratch)),
        out_shape=(
            jax.ShapeDtypeStruct((seq, width), BF16),
            jax.ShapeDtypeStruct((seq, width), F32),
            jax.ShapeDtypeStruct(packed.shape, BF16),
            jax.ShapeDtypeStruct((layers, VROWS, width), F32),
        ),
        in_specs=[pl.BlockSpec(memory_space=pltpu.SMEM)] + [vmem] * 4,
        out_specs=(vmem, vmem, pl.BlockSpec(memory_space=pl.ANY), vmem),
        scratch_shapes=list(scratch.values()),
        compiler_params=pltpu.CompilerParams(vmem_limit_bytes=63 * 2**20),
    )(lengths, tokens, cotangent, packed, vecs)


BOTH = ("dp", "fsdp")


def general(lengths, tokens, cotangent, vectors, weights):
    whole = lambda v, axis: lax.all_gather(v, BOTH, axis=axis, tiled=True)
    w_all = [whole(w, 1) for w in weights]
    v_all = [whole(v, v.ndim - 1) for v in vectors]
    layers, width, _ = w_all[1].shape
    groups = group_shape(width, w_all[2].shape[2])
    blocks = []
    for w in w_all[:3]:
        cut = w.reshape((layers,) + groups + (GROUP, -1, width))
        blocks.append(jnp.moveaxis(cut, -2, -3).reshape((layers,) + groups + (-1, width)))
    blocks.append(w_all[3].reshape((layers,) + groups + (-1, width)))
    vecs = jnp.concatenate([v.reshape(layers, -1, width) for v in v_all], axis=1).astype(F32)
    mixed, grad_tokens, grads, vgrads = plain(
        lengths, tokens, cotangent, jnp.concatenate(blocks, axis=-2), vecs
    )
    reduce = lambda g, axis: lax.psum_scatter(g, BOTH, scatter_dimension=axis, tiled=True)
    w_grads, first = [], 0
    for n, (w, block) in enumerate(zip(w_all, blocks)):
        part = grads[..., first : first + block.shape[-2], :].astype(F32)
        first += block.shape[-2]
        if n < 3:
            part = part.reshape((layers,) + groups + (-1, GROUP, width))
            part = jnp.moveaxis(part, -3, -2)
        w_grads.append(reduce(part.reshape(w.shape), 1))
    v_grads, first = [], 0
    for v in v_all:
        count = v.size // (layers * width)
        part = vgrads[:, first : first + count].reshape(v.shape)
        first += count
        v_grads.append(reduce(part, v.ndim - 1))
    return mixed, grad_tokens, v_grads, w_grads


def on_device(mesh, tokens, lengths, *rest):
    gains, shifts, w_qkv, b_qkv, w_attn, blends, w_in, b_in, w_out, biases, cotangent = rest
    vectors = (gains, shifts, b_qkv, blends, b_in, biases)
    weights = (w_qkv, w_attn, w_in, w_out)
    layers, _, width = w_attn.shape
    groups = group_shape(width, w_in.shape[2])
    if (mesh.shape["dp"], mesh.shape["fsdp"]) == (groups[0] * groups[1], groups[2] * groups[3]):
        mixed, grad_tokens, tile, *w_grads = fused(
            lengths, tokens, cotangent, vectors, weights
        )
        large, v_grads = finish(
            Vectors(layers, width, w_in.shape[2]),
            (mixed, grad_tokens, *w_grads),
            tile,
            [v.shape for v in vectors],
        )
        mixed, grad_tokens, *w_grads = large
    else:
        mixed, grad_tokens, v_grads, w_grads = general(
            lengths, tokens, cotangent, vectors, weights
        )
    d_gains, d_shifts, d_b_qkv, d_blends, d_b_in, d_biases = v_grads
    d_w_qkv, d_w_attn, d_w_in, d_w_out = w_grads
    return (
        mixed,
        grad_tokens,
        d_gains,
        d_shifts,
        d_w_qkv,
        d_b_qkv,
        d_w_attn,
        d_blends,
        d_w_in,
        d_b_in,
        d_w_out,
        d_biases,
    )


def solution(mesh):
    rows, vector = P(BOTH, None), P(None, None, BOTH)
    weight, bias = P(None, BOTH, None), P(None, BOTH)
    in_specs = (
        rows,
        P(BOTH),
        vector,
        vector,
        weight,
        bias,
        weight,
        vector,
        weight,
        bias,
        weight,
        vector,
        rows,
    )
    out_specs = (
        rows,
        rows,
        vector,
        vector,
        weight,
        bias,
        weight,
        vector,
        weight,
        bias,
        weight,
        vector,
    )
    return jax.shard_map(
        functools.partial(on_device, mesh),
        mesh=mesh,
        in_specs=in_specs,
        out_specs=out_specs,
        check_vma=False,
    )
```

profile of v0, /device:TPU:0, one launch (start us, length us, event | category | flops | bytes accessed | tf_op | source)
XLA Modules:
  0.0 144.8 jit_solution(11813091875945216658)
XLA Ops:
  0.6 0.0 copy-start.1
  1.3 0.0 copy-done.1
  1.3 0.6 copy.25.refs_5_
  1.9 137.6 %shard_map.220 = (bf16[512,512]{1,0:T(8,128)(2,1)}, f32[512,512]{1,0:T(8,128)}, f32[16,128]{1,0:T(8,128)}, f32[2,16,1536]{2,1,0:T(8,128)}, f32[2,16,512]{2,1,0:T...) custom-call(s32[1]{0:T(128)S(6)} %copy.27.length_ref, bf16[512,512]{1,0:T(8,128)(2,1)} %refs_0_.1, ...), custom_call_target="tpu_custom_call" | custom-call | tf_op jit(solution)/shard_map/pallas_call | solution.py:968
  139.5 4.0 %shard_map.221 = (bf16[512,512]{1,0:T(8,128)(2,1)}, f32[512,512]{1,0:T(8,128)}, f32[2,16,1536]{2,1,0:T(8,128)}, f32[2,16,512]{2,1,0:T(8,128)}, f32[2,16,2048]{2,...) custom-call(bf16[512,512]{1,0:T(8,128)(2,1)} %get-tuple-element.31.r, ...), custom_call_target="tpu_custom_call" | custom-call | tf_op jit(solution)/shard_map/pallas_call | solution.py:1009
  143.5 0.0 copy-start
  143.5 0.7 copy-done
  144.2 0.6 copy.26
Async XLA Ops:
  0.6 0.7 copy-start.1
  143.5 0.7 copy-start
where the time goes:
time: 145 us
  Pallas kernels  142 us (98%)
  local copies, waits for them, and re-layouts  1.85 us (1%)
    pallas_call x1, Pallas kernels, fused(): pl.pallas_call(functools.partial(fused_body, sizes, groups[0], tuple(scra...  138 us
    pallas_call x1, Pallas kernels, finish(): pl.pallas_call(functools.partial(finish_body, vectors, len(large)), out_s...  4.02 us

commit v1 on v0

--- a/solution.py
+++ b/solution.py
@@ -583,25 +583,29 @@
 
 ORDERS = {
     ("gather", 0): (
-        "xzy", "zyx", "zxy", "zyx", "yzx", "zxy",
-        "zyx", "zxy", "zyx", "zxy", "zyx", "zxy",
+        (2, "zyx"), (7, "zyx"), (5, "zxy"), (1, "zyx"),
+        (8, "zxy"), (0, "zyx"), (4, "zyx"), (10, "zyx"),
+        (3, "xzy"), (9, "zxy"), (11, "xzy"), (6, "zxy"),
     ),
     ("gather", 1): (
-        "zyx", "xzy", "yzx", "yzx", "zyx", "xzy",
-        "yzx", "zxy", "zyx", "zyx", "xzy", "xzy",
+        (2, "zxy"), (6, "zyx"), (0, "yzx"), (1, "yzx"),
+        (3, "xzy"), (7, "xzy"), (4, "yzx"), (5, "xzy"),
+        (9, "zxy"), (10, "yzx"), (8, "zyx"), (11, "xzy"),
     ),
     ("scatter", 0): (
-        "xyz", "xyz", "yzx", "xyz", "xyz", "yxz",
-        "xyz", "yxz", "xzy", "yzx", "yzx", "xyz",
+        (6, "xzy"), (9, "xzy"), (2, "xyz"), (8, "yxz"),
+        (11, "yxz"), (10, "xzy"), (3, "yxz"), (5, "yxz"),
+        (0, "xyz"), (4, "yxz"), (7, "yzx"), (1, "yxz"),
     ),
     ("scatter", 1): (
-        "yxz", "xzy", "yzx", "yxz", "xzy", "yzx",
-        "xyz", "xyz", "xyz", "xyz", "yzx", "yzx",
+        (1, "xzy"), (0, "xzy"), (5, "yzx"), (7, "yxz"),
+        (4, "yxz"), (9, "yxz"), (6, "xyz"), (10, "xzy"),
+        (2, "yxz"), (3, "xzy"), (11, "yzx"), (8, "xzy"),
     ),
 }
-LINK, HOP = 0.0235, 1.8
+LINK, HOP = 0.0235, 2.0
 CORE, CORE_HOP = 0.0027, 0.9
-ISSUE, BACKLOG, AHEAD = 0.04, 6.0, 12
+ISSUE, BACKLOG, AHEAD = 0.04, 5.0, 13
 
 
 def plan(layers, segments, parts):
@@ -686,12 +690,11 @@
     units = rows // GROUP
     parts = {("gather", 0, "vectors"): (4, "zxy", False)}
     for l in range(layers):
-        for u in range(units):
-            parts["gather", l, u] = (GROUP, ORDERS["gather", l][u], False)
-    late = list(range(units - ff, units)) + list(range(4, units - ff)) + [3, 2, 1, 0]
+        for u, order in ORDERS["gather", l]:
+            parts["gather", l, u] = (GROUP, order, False)
     for l in reversed(range(layers)):
-        for u in late:
-            parts["scatter", l, u] = (GROUP, ORDERS["scatter", l][u], True)
+        for u, order in ORDERS["scatter", l]:
+            parts["scatter", l, u] = (GROUP, order, True)
     parts["scatter", 0, "vectors"] = (8, "yxz", True)
     gathers = lambda l, us: [("gather", l, u) for u in us]
     scatters = lambda l, us: [("scatter", l, u) for u in us]

time: 145 us -> 139 us (0.959)
  Pallas kernels: 142 us -> 136 us
    pallas_call x1, Pallas kernels: 138 us -> 132 us  [fused(): pl.pallas_call(functools.partial(fused_body, sizes, groups[0], tuple(scra...]
where the time goes in v1:
time: 139 us
  Pallas kernels  136 us (98%)
  local copies, waits for them, and re-layouts  1.85 us (1%)
    pallas_call x1, Pallas kernels, fused(): pl.pallas_call(functools.partial(fused_body, sizes, groups[0], tuple(scra...  132 us
    pallas_call x1, Pallas kernels, finish(): pl.pallas_call(functools.partial(finish_body, vectors, len(large)), out_s...  4.02 us

profile of v1, /device:TPU:0, one launch (start us, length us, event | category | flops | bytes accessed | tf_op | source)
XLA Modules:
  0.0 139.2 jit_solution(800659504625824460)
XLA Ops:
  0.6 0.0 copy-start.1
  1.3 0.0 copy-done.1
  1.3 0.6 copy.25.refs_5_
  1.9 132.0 %shard_map.220 = (bf16[512,512]{1,0:T(8,128)(2,1)}, f32[512,512]{1,0:T(8,128)}, f32[16,128]{1,0:T(8,128)}, f32[2,16,1536]{2,1,0:T(8,128)}, f32[2,16,512]{2,1,0:T...) custom-call(s32[1]{0:T(128)S(6)} %copy.27.length_ref, bf16[512,512]{1,0:T(8,128)(2,1)} %refs_0_.1, ...), custom_call_target="tpu_custom_call" | custom-call | tf_op jit(solution)/shard_map/pallas_call | solution.py:971
  133.9 4.0 %shard_map.221 = (bf16[512,512]{1,0:T(8,128)(2,1)}, f32[512,512]{1,0:T(8,128)}, f32[2,16,1536]{2,1,0:T(8,128)}, f32[2,16,512]{2,1,0:T(8,128)}, f32[2,16,2048]{2,...) custom-call(bf16[512,512]{1,0:T(8,128)(2,1)} %get-tuple-element.31.r, ...), custom_call_target="tpu_custom_call" | custom-call | tf_op jit(solution)/shard_map/pallas_call | solution.py:1012
  137.9 0.0 copy-start
  138.0 0.7 copy-done
  138.6 0.6 copy.26
Async XLA Ops:
  0.6 0.7 copy-start.1
  137.9 0.7 copy-start

commit v2 on v1

--- a/solution.py
+++ b/solution.py
@@ -781,8 +781,12 @@
         table[...] = jnp.zeros_like(table)
         for l in range(self.layers):
             for ref, row in zip(refs, VECTOR_ROWS):
+                turned = row == BLEND
                 row += l * VROWS
-                if len(ref.shape) == 3:
+                if turned:
+                    for n in range(ref.shape[0]):
+                        table[row + n : row + n + 1, :GROUP] = ref[n, l : l + 1, :].astype(F32)
+                elif len(ref.shape) == 3:
                     table[row : row + ref.shape[1], :GROUP] = ref[l].astype(F32)
                 else:
                     value = ref[l : l + 1, :].astype(F32)
@@ -796,8 +800,12 @@
         table[...] = jnp.concatenate([tile, rest], axis=0).T
         for l in range(self.layers):
             for ref, row in zip(refs, VECTOR_ROWS):
+                turned = row == BLEND
                 row += l * VROWS
-                if len(ref.shape) == 3:
+                if turned:
+                    for n in range(ref.shape[0]):
+                        ref[n, l : l + 1, :] = table[row + n : row + n + 1, :GROUP]
+                elif len(ref.shape) == 3:
                     ref[l] = table[row : row + ref.shape[1], :GROUP]
                 else:
                     count = ref.shape[1] // GROUP
@@ -1136,6 +1144,8 @@
     layers, _, width = w_attn.shape
     groups = group_shape(width, w_in.shape[2])
     if (mesh.shape["dp"], mesh.shape["fsdp"]) == (groups[0] * groups[1], groups[2] * groups[3]):
+        turn = lambda vs: [v.transpose(1, 0, 2) if n == 3 else v for n, v in enumerate(vs)]
+        vectors = turn(vectors)
         mixed, grad_tokens, tile, *w_grads = fused(
             lengths, tokens, cotangent, vectors, weights
         )
@@ -1146,6 +1156,7 @@
             [v.shape for v in vectors],
         )
         mixed, grad_tokens, *w_grads = large
+        v_grads = turn(v_grads)
     else:
         mixed, grad_tokens, v_grads, w_grads = general(
             lengths, tokens, cotangent, vectors, weights

time: 139 us -> 138 us (level)
  local copies, waits for them, and re-layouts: 1.85 us -> 0 us
    unnamed x6 -> x0, local copies, waits for them, and re-layouts: 1.85 us -> none
where the time goes in v2:
time: 138 us
  Pallas kernels  136 us (99%)
  between operations  1.5 us (1%)
    pallas_call x1, Pallas kernels, fused(): pl.pallas_call(functools.partial(fused_body, sizes, groups[0], tuple(scra...  132 us
    pallas_call x1, Pallas kernels, finish(): pl.pallas_call(functools.partial(finish_body, vectors, len(large)), out_s...  4.02 us

profile of v2, /device:TPU:0, one launch (start us, length us, event | category | flops | bytes accessed | tf_op | source)
XLA Modules:
  0.0 137.6 jit_solution(2256772396021729345)
XLA Ops:
  1.3 132.0 %shard_map.220 = (bf16[512,512]{1,0:T(8,128)(2,1)}, f32[512,512]{1,0:T(8,128)}, f32[16,128]{1,0:T(8,128)}, f32[2,16,1536]{2,1,0:T(8,128)}, f32[2,16,512]{2,1,0:T...) custom-call(s32[1]{0:T(128)S(6)} %copy.25.length_ref, bf16[512,512]{1,0:T(8,128)(2,1)} %refs_0_.1, ...), custom_call_target="tpu_custom_call" | custom-call | tf_op jit(solution)/shard_map/pallas_call | solution.py:979
  133.3 4.0 %shard_map.221 = (bf16[512,512]{1,0:T(8,128)(2,1)}, f32[512,512]{1,0:T(8,128)}, f32[2,16,1536]{2,1,0:T(8,128)}, f32[2,16,512]{2,1,0:T(8,128)}, f32[2,16,2048]{2,...) custom-call(bf16[512,512]{1,0:T(8,128)(2,1)} %get-tuple-element.31.r, ...), custom_call_target="tpu_custom_call" | custom-call | tf_op jit(solution)/shard_map/pallas_call | solution.py:1020
